TPU v7x, 128 devices: a whole 4x4x4 slice. The times are simulated.
128 devices in a mesh: dp: 8 (over z, core), table: 16 (over x, y).
Axes of the slice: x: 4, y: 4, z: 4, core: 2. Of those that a mesh axis runs over, the one named last changes fastest.
Arguments:
- emb_table: bfloat16 [32768, 128, 128], P(('dp', 'table')), may hold values from -6 to 6
- requests: int32 [16384, 3], P(('dp', 'table')), may hold values from -1 to 255, as said below
- bag_rows: int32 [16777216], P(('dp', 'table')), may hold values from 0 to 49151, as said below
- placement_slot: int32 [524288], P(('dp', 'table')), may hold values from -1 to 2047, as said below
- w_hidden: bfloat16 [2048, 1024], replicated, may hold values from -0.125 to 0.125
- w_out: bfloat16 [1024, 256], replicated, may hold values from -0.1875 to 0.1875
Outputs:
- item_vectors: bfloat16 [262144, 256], P(('dp', 'table'))
Inputs may be any that keep to these rules, and one draw needn't show every extreme that they name: `placement_slot`: each device's slots hold -1 for items that are not dirty, else k * 256 + s, sending the item to slot s of index shard k (the device of dp index k in the same table column). No value repeats on one device, the slots s used toward each k run from 0 upward, and in each table column one index shard gets 256 items from every device. In each row (one device, one owner) the live block numbers come first and the -1 entries after them; every device has some owner from which it requests 3 blocks, and owners differ in how many blocks are asked of them. `bag_rows`: every entry names a row of a block slot whose request is not -1.
All inputs are finite; a program needn't handle non-finite values.
Results may differ from a plain program's by a relative error of at most 0.0059.
Values may be sent and summed in bfloat16 or wider, within the bound.
A program may use at most 128 MiB of HBM per device.

v0:
```python
import jax
import jax.numpy as jnp
from jax import lax
from jax.sharding import PartitionSpec as P

FEATS = 16
BAG = 2


def item_tower(inputs, w_hidden, w_out):
    hidden = jnp.maximum(jnp.dot(inputs, w_hidden, preferred_element_type=jnp.float32), 0.0).astype(
        jnp.bfloat16
    )
    raw = jnp.dot(hidden, w_out, preferred_element_type=jnp.float32)
    scale = lax.rsqrt(jnp.mean(raw * raw, axis=-1, keepdims=True) + 1e-06)
    return (raw * scale).astype(jnp.bfloat16)


def serve_local(emb_table, block_ids):
    served = jnp.take(emb_table, jnp.maximum(block_ids, 0), axis=0)
    live = (block_ids >= 0)[..., None, None]
    return jnp.where(live, served, jnp.zeros_like(served))


def invert_slots(placement_slot, slot_count):
    item_count = placement_slot.shape[0]
    step_rows = min(512, slot_count)
    block_count = slot_count // step_rows
    item_iota = jnp.arange(item_count, dtype=jnp.int32)[None, :]

    def one_block(start):
        wanted = start + jnp.arange(step_rows, dtype=jnp.int32)[:, None]
        match = placement_slot[None, :] == wanted
        source = jnp.sum(jnp.where(match, item_iota, 0), axis=1)
        present = jnp.any(match, axis=1)
        return (source, present)

    starts = jnp.arange(block_count, dtype=jnp.int32) * step_rows
    source, present = lax.map(one_block, starts)
    return (source.reshape(slot_count), present.reshape(slot_count))


def local(emb_table, requests, bag_rows, placement_slot, w_hidden, w_out):
    dp_count = lax.axis_size("dp")
    table_count = lax.axis_size("table")
    device_count = dp_count * table_count
    block_cap = requests.shape[1]
    block_rows = emb_table.shape[1]
    emb_width = emb_table.shape[2]
    width = FEATS * emb_width
    out_width = w_out.shape[1]
    served = serve_local(
        emb_table,
        lax.all_to_all(requests, ("dp", "table"), split_axis=0, concat_axis=0, tiled=True),
    )
    fetched = lax.all_to_all(served, ("dp", "table"), split_axis=0, concat_axis=0, tiled=True)
    fetched_rows = fetched.reshape(device_count * block_cap * block_rows, emb_width)
    item_count = placement_slot.shape[0]
    send_cap = item_count // (2 * dp_count)
    slot_count = dp_count * send_cap
    source, present = invert_slots(placement_slot, slot_count)
    bag_matrix = bag_rows.reshape(item_count, FEATS * BAG)
    slot_bags = jnp.take(bag_matrix, source, axis=0).reshape(-1)
    picked = jnp.take(fetched_rows, slot_bags, axis=0).reshape(slot_count, FEATS, BAG, emb_width)
    pooled = jnp.sum(picked, axis=2, dtype=jnp.float32).reshape(slot_count, width)
    outgoing = jnp.where(present[:, None], pooled, 0.0).astype(jnp.bfloat16)
    local_vectors = item_tower(outgoing, w_hidden, w_out)
    local_vectors = local_vectors.reshape(dp_count, send_cap, out_width)
    vectors = lax.all_to_all(local_vectors, "dp", split_axis=0, concat_axis=0, tiled=True)
    return vectors.reshape(dp_count * send_cap, out_width)


def solution(mesh):
    placed = (
        P(("dp", "table"), None, None),
        P(("dp", "table"), None),
        P(("dp", "table")),
        P(("dp", "table")),
        P(),
        P(),
    )
    return jax.shard_map(
        local, mesh=mesh, in_specs=placed, out_specs=P(("dp", "table"), None), check_vma=False
    )
```

profile of v0, /device:TPU:26, one launch (start us, length us, event | category | flops | bytes accessed | tf_op | source)
XLA Modules:
  0.0 583.4 jit_solution(16316276343126414753)
XLA Ops:
  0.0 1.5 copy.33
  1.5 10.3 %all-to-all-start = ((s32[128,1,3]{2,1,0:T(1,128)}), s32[128,1,3]{2,1,0:T(1,128)S(1)}, u32[]{:S(2)}, u32[]{:S(2)}) async-start(s32[128,1,3]{2,1,0:T(1,128)} %bitcast.1), calls=%async_computation | async-start | bytes 131072 | tf_op jit(solution)/shard_map/all_to_all | solution.py:54
  11.8 20.8 %while.13 = (s32[]{:T(128)}, s32[4,512]{1,0:T(4,128)S(1)}, pred[4,512]{1,0:T(4,128)(4,1)S(1)}, s32[4096]{0:T(1024)}, s32[4]{0:T(128)S(1)}, /*index=5*/s32[]{:T(128)}, s32[]{:T(128)}) while((s32[]{:T(128)}, s32[4,512]{1,0:T(4,128)S(1)}, pred[4,512]{1,0:T(4,128)(4,1)S(1)}, s32[4096]{0:T(1024)}, s32[4]{0:T(128)S(1)}, ...), condition=%wide.region_3.4_spmd.clone, body=%wide.region_0.3_spmd.clone.sunk | while | flops 10485250 | bytes 47717 | solution.py:39
  11.8 0.6 dynamic_slice.6
  12.4 0.6 iota_add_fusion.2
  13.0 2.0 fusion.21
  15.0 1.9 compare_reduce_fusion.2
  17.0 0.6 dynamic_slice.6
  17.6 0.6 iota_add_fusion.2
  18.2 2.0 fusion.21
  20.2 1.9 compare_reduce_fusion.2
  22.2 0.6 dynamic_slice.6
  22.8 0.6 iota_add_fusion.2
  23.4 2.0 fusion.21
  25.4 1.9 compare_reduce_fusion.2
  27.4 0.6 dynamic_slice.6
  28.6 2.0 fusion.21
  30.6 1.9 compare_reduce_fusion.2
  32.6 1.6 reshape.150
  34.3 7.6 %gather_fusion = s32[2048,32]{1,0:T(8,128)} fusion(s32[4096,32]{1,0:T(8,128)S(1)} %reshape.150, s32[2048]{0:T(1024)S(1)} %broadcast_clamp_fusion.1), kind=kCustom, calls=%fused_computation | custom fusion | bytes 532480 | tf_op jit(solution)/shard_map/jit(_take)/gather | solution.py:63
  41.9 1.5 copy.31
  43.4 1.6 broadcast_select_fusion.1
  46.0 10.5 %copy.32 = pred[2048,16,2]{2,1,0:T(8,128)(4,1)} copy(pred[2048,16,2]{0,2,1:T(4,128)(4,1)S(1)} %compare_and_fusion) | data formatting | bytes 131072 | tf_op jit(solution)/shard_map/jit(_take)/and | solution.py:64
  57.3 14.5 %gather_fusion.1 = bf16[384,128,128]{2,1,0:T(8,128)(2,1)} fusion(bf16[256,128,128]{2,1,0:T(8,128)(2,1)} %param.8, s32[1024]{0:T(1024)S(1)} %pad_clamp_fusion), kind=kCustom, calls=%fused_computation.1 | custom fusion | bytes 25167360 | tf_op jit(solution)/shard_map/jit(_take)/gather | solution.py:20
  71.7 10.9 %select_select_fusion = bf16[128,3,128,128]{3,2,1,0:T(8,128)(2,1)} fusion(bf16[128,3,128,128]{3,2,1,0:T(8,128)(2,1)} %bitcast.43, pred[128,3]{1,0:T(8,128)(4,1)S(1)} %bitcast.49, pred[128,3]{1,0:T(8,128)(4,1)S(1)} %bitcast.48), kind=kLoop, calls=%fused_computation.12 | loop fusion | flops 12582912 | bytes 25166592 | tf_op jit(solution)/shard_map/jit(_where)/select_n | solution.py:22
  82.6 10.2 %all-to-all-start.1 = ((bf16[128,3,128,128]{3,2,1,0:T(8,128)(2,1)}), bf16[128,3,128,128]{3,2,1,0:T(8,128)(2,1)}, u32[]{:S(2)}, u32[]{:S(2)}) async-start(bf16[128,3,128,128]{3,2,1,0:T(8,128)(2,1)} %select_select_fusion), calls=%async_computation.1 | async-start | bytes 25165824 | tf_op jit(solution)/shard_map/all_to_all | solution.py:56
  93.2 167.7 %all-to-all-done.1 = bf16[128,3,128,128]{3,2,1,0:T(8,128)(2,1)} async-done(((bf16[128,3,128,128]{3,2,1,0:T(8,128)(2,1)}), bf16[128,3,128,128]{3,2,1,0:T(8,128)(2,1)}, u32[]{:S(2)}, u32[]{:S(2)}) %all-to-all-start.1) | async-done | bytes 12582944 | tf_op jit(solution)/shard_map/all_to_all | solution.py:56
  260.8 223.9 %gather_fusion.2 = bf16[65536,128]{1,0:T(8,128)(2,1)} fusion(bf16[49152,128]{1,0:T(8,128)(2,1)} %bitcast.5, s32[65536]{0:T(1024)S(1)} %broadcast_clamp_fusion), kind=kCustom, calls=%fused_computation.2 | custom fusion | bytes 33816576 | tf_op jit(solution)/shard_map/jit(_take)/gather | solution.py:64
  484.7 64.3 %convert_reduce_fusion = bf16[2048,16,128]{2,1,0:T(8,128)(2,1)} fusion(bf16[2048,16,2,128]{3,2,1,0:T(2,128)(2,1)} %bitcast.42, pred[2048,16,2]{2,1,0:T(8,128)(4,1)} %copy.32), kind=kLoop, calls=%fused_computation.8 | loop fusion | flops 20971520 | bytes 25231360 | tf_op jit(solution)/shard_map/reduce_sum | solution.py:65
  549.1 14.5 %multiply_reduce_fusion = (f32[2048]{0:T(1024)S(1)}, f32[2048,256]{1,0:T(8,128)S(1)}) fusion(bf16[1024,256]{1,0:T(8,128)(2,1)S(1)} %copy-done, bf16[2048,1024]{1,0:T(8,128)(2,1)} %param.12, bf16[256,8,16,128]{3,2,1,0:T(8,128)(2,1)} %bitcast.44, pred[2048]{0:T(1024)(128)(4,1)S(1)} %bitcast.56), kind=kOutput, calls=%fused_computation.20 | convolution fusion | flops 9673111552 | bytes 15214592 | tf_op jit(solution)/shard_map/dot_general | solution.py:14
  564.0 18.5 %all_to_all.19 = bf16[8,256,256]{2,1,0:T(8,128)(2,1)S(1)} all-to-all(bf16[8,256,256]{2,1,0:T(8,128)(2,1)S(1)} %bitcast.45), channel_id=1, replica_groups=mesh['dp'=8,'table'=16] {'dp'}, dimensions={0} | all-to-all | bytes 2097152 | tf_op jit(solution)/shard_map/all_to_all | solution.py:69
  582.5 1.0 copy.65
  (40 shorter events, 3.4 us)
Async XLA Ops:
  0.0 549.1 %copy-start = (bf16[1024,256]{1,0:T(8,128)(2,1)S(1)}, bf16[1024,256]{1,0:T(8,128)(2,1)}, u32[]{:S(2)}) copy-start(bf16[1024,256]{1,0:T(8,128)(2,1)} %param.13) | copy-start | bytes 1572868
  1.5 55.1 %all-to-all-start = ((s32[128,1,3]{2,1,0:T(1,128)}), s32[128,1,3]{2,1,0:T(1,128)S(1)}, u32[]{:S(2)}, u32[]{:S(2)}) async-start(s32[128,1,3]{2,1,0:T(1,128)} %bitcast.1), calls=%async_computation | async-start | bytes 131072 | tf_op jit(solution)/shard_map/all_to_all | solution.py:54
  82.6 178.2 %all-to-all-start.1 = ((bf16[128,3,128,128]{3,2,1,0:T(8,128)(2,1)}), bf16[128,3,128,128]{3,2,1,0:T(8,128)(2,1)}, u32[]{:S(2)}, u32[]{:S(2)}) async-start(bf16[128,3,128,128]{3,2,1,0:T(8,128)(2,1)} %select_select_fusion), calls=%async_computation.1 | async-start | bytes 25165824 | tf_op jit(solution)/shard_map/all_to_all | solution.py:56
where the time goes:
time: 590 us; the launch traced here: 583 us
  local copies, waits for them, and re-layouts  266 us (45%)
  waiting for transfers between devices  168 us (28%)
  other arithmetic  95.7 us (16%)
  starting transfers between devices  20.5 us (3%)
  blocking collectives  18.5 us (3%)
  matrix products  14.5 us (2%)
    gather x1, local copies, waits for them, and re-layouts, local(): jnp.take(fetched_rows, slot_bags, axis=0)  224 us
    all_to_all x1, waiting for transfers between devices, local(): lax.all_to_all(served, ('dp', 'table'), split_axis=0, concat_axis=0, tile...  168 us
    reduce_sum x1, other arithmetic, local(): jnp.sum(picked, axis=2, dtype=jnp.float32).reshape(slot_count, width)  64.3 us
    all_to_all x1, blocking collectives, local(): lax.all_to_all(local_vectors, 'dp', split_axis=0, concat_axis=0, tiled=True)  18.5 us
    dot_general x1, matrix products, item_tower(): raw = jnp.dot(hidden, w_out, preferred_element_type=jnp.float32)  14.5 us
    gather x1, local copies, waits for them, and re-layouts, serve_local(): served = jnp.take(emb_table, jnp.maximum(block_ids, 0), axis=0)  14.5 us
  transfers between devices with their start and end apart: 2, of which 1 were waited for; matrix products, arithmetic and copies ran while one was open for 8% of the time, Pallas kernels for 0%

commit v1 on v0

v1 whole, which is shorter than its diff:
```python
import itertools

import jax
import jax.numpy as jnp
import numpy as np
from jax import lax
from jax.experimental import pallas as pl
from jax.experimental.pallas import tpu as pltpu
from jax.sharding import PartitionSpec as P

MESH = pl.DeviceIdType.MESH
FEATS = 16
N_DP, N_TABLE = 8, 16
DEVICES = N_DP * N_TABLE
CAP = 3
ROWS = 128
EMB = 128
ITEMS = 4096
SLOTS = 2048
GROUP = 256
GROUPS = SLOTS * FEATS // GROUP
SHARD = SLOTS // N_DP
UNITS = 1024
VEC = 256
TABLE_ROWS = CAP * DEVICES * ROWS
ZERO_ROW = TABLE_ROWS

DISPLACEMENTS = [d for d in itertools.product(range(4), range(4), range(4), range(2)) if any(d)]


def hops(d):
    load = np.zeros(6)
    for axis in range(3):
        if d[axis] in (1, 2):
            load[2 * axis] += 1
        if d[axis] in (2, 3):
            load[2 * axis + 1] += 1
    return load


def balanced(left):
    left, out, total = list(left), [], np.zeros(6)
    mean = sum(hops(d).sum() for d in left) / len(left)
    rng = np.random.default_rng(0)

    def score(d):
        after = total + hops(d)
        value = 10 * (after.max() - after.min()) + ((after - after.mean()) ** 2).sum()
        return value + 0.3 * abs(after.sum() / (len(out) + 1) - mean) + 0.01 * rng.random()

    while left:
        best = min([(score(d), d) for d in left])[1]
        left.remove(best)
        out.append(best)
        total = total + hops(best)
    return out


def part_of(d):
    return ((d[1] - d[0]) % 4) * 2 + d[3]


def place_of(d):
    return part_of(d) * 16 + d[0] * 4 + (d[2] - d[0]) % 4


ORDER = balanced(DISPLACEMENTS)
ORDER_BY_PART = sum([balanced([d for d in DISPLACEMENTS if part_of(d) == k]) for k in range(8)], [])


def my_place():
    i, j = lax.axis_index("dp"), lax.axis_index("table")
    return lax.div(j, 4), lax.rem(j, 4), lax.div(i, 2), lax.rem(i, 2)


def moved(d, sign):
    x, y, z, core = my_place()
    x = lax.rem(x + (sign * d[0]) % 4, 4)
    y = lax.rem(y + (sign * d[1]) % 4, 4)
    z = lax.rem(z + (sign * d[2]) % 4, 4)
    core = lax.rem(core + d[3], 2)
    return z * 2 + core, x * 4 + y


def table_row(idx, present):
    x, y, z, core = my_place()
    block = idx >> 7
    owner = (block * 43691) >> 17
    slot = block - owner * 3
    dx = (x - ((owner >> 2) & 3)) & 3
    dy = (y - (owner & 3)) & 3
    dz = (z - (owner >> 5)) & 3
    dcore = (core - ((owner >> 4) & 1)) & 1
    part = ((dy - dx) & 3) * 2 + dcore
    place = part * 16 + dx * 4 + ((dz - dx) & 3)
    row = ((slot * DEVICES + place) << 7) | (idx & 127)
    return jnp.where(present, row, ZERO_ROW), jnp.where(present, jnp.where(slot == 2, slot + part, slot), 0)


def pick_bags(bags_ref, placed_ref, bag_t, picked):
    bag_t[...] = jnp.transpose(bags_ref[...])
    ones = jnp.ones((8, 1024), jnp.float32)

    def chunk(n, _):
        lane = lax.broadcasted_iota(jnp.int32, (1024, 256), 1) + n * 256
        wanted = (lane & 127) * 16 + (lane >> 7)
        total = jnp.zeros((72, 256), jnp.float32)
        for q in range(4):
            hit = placed_ref[:, q : q + 1] == wanted
            hit = jnp.where(hit, 1.0, 0.0).astype(jnp.bfloat16)
            bag = bag_t[q * 32 : (q + 1) * 32, :]
            left = jnp.concatenate([(bag >> 8).astype(jnp.float32), (bag & 255).astype(jnp.float32), ones])
            total += jnp.dot(left.astype(jnp.bfloat16), hit, preferred_element_type=jnp.float32)
        picked[2 * n] = total[:, :128]
        picked[2 * n + 1] = total[:, 128:]
        return 0

    lax.fori_loop(0, SLOTS // 256, chunk, 0)


def bag_matrix(picked, entry):
    rows, live = [], []
    for t in range(16):
        high = picked[t, pl.ds(entry, 16, stride=2), :]
        low = picked[t, pl.ds(32 + entry, 16, stride=2), :]
        rows.append(high.astype(jnp.int32) * 256 + low.astype(jnp.int32))
        there = picked[t, 64:72, :] > 0.5
        live.append(jnp.concatenate([jnp.where(there, 1, 0)] * 2))
    return jnp.concatenate(rows), jnp.concatenate(live) > 0


def fetch_kernel(
    emb, req, bags, placed, fetched, row_a, row_b,
    emb_v, staged, req_in, req_s, bag_t, picked,
    emb_sem, req_send, req_recv, own_sem, send_sem, recv_sem,
):
    me_dp, me_table = lax.axis_index("dp"), lax.axis_index("table")
    load = pltpu.make_async_copy(emb, emb_v, emb_sem)
    load.start()
    barrier = pltpu.get_barrier_semaphore()
    for d in ORDER:
        pl.semaphore_signal(barrier, inc=1, device_id=moved(d, 1), device_id_type=MESH)
    pl.semaphore_wait(barrier, DEVICES - 1)

    own = pltpu.make_async_copy(req.at[me_dp * N_TABLE + me_table], req_in.at[0], own_sem)
    own.start()
    for d in ORDER:
        to = moved(d, -1)
        pltpu.make_async_remote_copy(
            src_ref=req.at[to[0] * N_TABLE + to[1]], dst_ref=req_in.at[place_of(d)],
            send_sem=req_send, recv_sem=req_recv, device_id=to, device_id_type=MESH,
        ).start()
    own.wait()
    others = req_in.at[pl.ds(1, DEVICES - 1)]
    pltpu.make_async_copy(others, others, req_recv).wait()
    pltpu.make_async_copy(others, others, req_send).wait()
    numbers = pltpu.make_async_copy(req_in, req_s, own_sem)
    numbers.start()
    load.wait()
    numbers.wait()

    for slot in range(CAP):

        def serve(n, _):
            number = req_s[n, 0, slot]
            block = emb_v[jnp.maximum(number, 0)]
            staged[slot, n] = jnp.where(number >= 0, block, jnp.zeros_like(block))
            return 0

        lax.fori_loop(0, DEVICES, serve, 0)
        for d in ORDER if slot < 2 else ORDER_BY_PART:
            n = place_of(d)
            pltpu.make_async_remote_copy(
                src_ref=staged.at[slot, n], dst_ref=fetched.at[slot, n],
                send_sem=send_sem, recv_sem=recv_sem, device_id=moved(d, 1), device_id_type=MESH,
            ).start()
    mine = pltpu.make_async_copy(staged.at[:, 0], fetched.at[:, 0], own_sem)
    mine.start()

    pick_bags(bags, placed, bag_t, picked)
    for entry, out in ((0, row_a), (1, row_b)):
        idx, present = bag_matrix(picked, entry)
        out[...] = table_row(idx, present)[0]

    mine.wait()
    arrived = fetched.at[:, pl.ds(1, DEVICES - 1)]
    pltpu.make_async_copy(arrived, arrived, recv_sem).wait()
    sent = staged.at[:, pl.ds(1, DEVICES - 1)]
    pltpu.make_async_copy(sent, sent, send_sem).wait()


def fetch(emb_table, requests, bag_rows, placement_slot):
    req = jnp.pad(requests, ((0, 0), (0, 125))).reshape(DEVICES, 1, 128)
    hbm = pl.BlockSpec(memory_space=pl.ANY)
    vmem = pl.BlockSpec(memory_space=pltpu.VMEM)
    return pl.pallas_call(
        fetch_kernel,
        in_specs=[hbm, vmem, vmem, vmem],
        out_specs=(hbm, vmem, vmem),
        out_shape=(
            jax.ShapeDtypeStruct((CAP, DEVICES, ROWS, EMB), jnp.bfloat16),
            jax.ShapeDtypeStruct((GROUP, GROUPS), jnp.int32),
            jax.ShapeDtypeStruct((GROUP, GROUPS), jnp.int32),
        ),
        scratch_shapes=[
            pltpu.VMEM((256, ROWS, EMB), jnp.bfloat16),
            pltpu.VMEM((CAP, DEVICES, ROWS, EMB), jnp.bfloat16),
            pltpu.VMEM((DEVICES, 1, 128), jnp.int32),
            pltpu.SMEM((DEVICES, 1, 128), jnp.int32),
            pltpu.VMEM((128, 1024), jnp.int32),
            pltpu.VMEM((16, 72, 128), jnp.float32),
        ]
        + [pltpu.SemaphoreType.DMA] * 6,
        compiler_params=pltpu.CompilerParams(
            collective_id=1, has_side_effects=True, vmem_limit_bytes=58 * 2**20
        ),
        name="fetch_blocks",
    )(emb_table, req, bag_rows.reshape(1024, 128), placement_slot.reshape(1024, 4))


def tower(x, w_hidden, w_out):
    hidden = jnp.maximum(jnp.dot(x, w_hidden, preferred_element_type=jnp.float32), 0.0).astype(jnp.bfloat16)
    raw = jnp.dot(hidden, w_out, preferred_element_type=jnp.float32)
    scale = lax.rsqrt(jnp.mean(raw * raw, axis=-1, keepdims=True) + 1e-06)
    return (raw * scale).astype(jnp.bfloat16)


def pool_kernel(row_a, row_b, fetched, w_hidden, w_out, out, table, rows, x, chunk, sem):
    step = pl.program_id(0)

    @pl.when(step == 0)
    def _():
        table[pl.ds(ZERO_ROW, 8), :] = jnp.zeros((8, EMB), jnp.float32)
        pieces = CAP * DEVICES // 16

        def copy(n):
            return pltpu.make_async_copy(
                fetched.at[lax.div(n, 8), pl.ds(lax.rem(n, 8) * 16, 16)], chunk.at[lax.rem(n, 2)], sem.at[lax.rem(n, 2)]
            )

        copy(0).start()

        def load(n, _):
            @pl.when(n + 1 < pieces)
            def _():
                copy(n + 1).start()

            copy(n).wait()
            for k in range(16):
                at = pl.multiple_of((n * 16 + k) * ROWS, ROWS)
                table[pl.ds(at, ROWS), :] = chunk[lax.rem(n, 2), k].astype(jnp.float32)
            return 0

        lax.fori_loop(0, pieces, load, 0)

    def group(g, _):
        def some(t, _):
            for f in range(FEATS):
                a = row_a[t * FEATS + f, step * 16 + g]
                b = row_b[t * FEATS + f, step * 16 + g]
                rows[pl.ds(f * 16 + t, 1), :] = table[pl.ds(a, 1), :] + table[pl.ds(b, 1), :]
            return 0

        lax.fori_loop(0, 16, some, 0, unroll=2)
        at = pl.multiple_of(g * 16, 16)
        for f in range(FEATS):
            x[pl.ds(at, 16), f * EMB : (f + 1) * EMB] = rows[f * 16 : (f + 1) * 16, :].astype(jnp.bfloat16)
        return 0

    lax.fori_loop(0, 16, group, 0)
    out[...] = tower(x[...], w_hidden[...], w_out[...])


def pool(row_a, row_b, fetched, w_hidden, w_out):
    smem = pl.BlockSpec(memory_space=pltpu.SMEM)
    return pl.pallas_call(
        pool_kernel,
        grid=(N_DP,),
        in_specs=[
            smem,
            smem,
            pl.BlockSpec(memory_space=pl.ANY),
            pl.BlockSpec((2048, UNITS), lambda n: (0, 0), pipeline_mode=pl.Buffered(1)),
            pl.BlockSpec((UNITS, VEC), lambda n: (0, 0), pipeline_mode=pl.Buffered(1)),
        ],
        out_specs=pl.BlockSpec((SHARD, VEC), lambda n: (n, 0)),
        out_shape=jax.ShapeDtypeStruct((SLOTS, VEC), jnp.bfloat16),
        scratch_shapes=[
            pltpu.VMEM((TABLE_ROWS + 8, EMB), jnp.float32),
            pltpu.VMEM((GROUP, EMB), jnp.float32),
            pltpu.VMEM((SHARD, FEATS * EMB), jnp.bfloat16),
            pltpu.VMEM((2, 16, ROWS, EMB), jnp.bfloat16),
            pltpu.SemaphoreType.DMA((2,)),
        ],
        compiler_params=pltpu.CompilerParams(vmem_limit_bytes=58 * 2**20),
        name="pool_and_tower",
    )(row_a, row_b, fetched, w_hidden, w_out)


def local(emb_table, requests, bag_rows, placement_slot, w_hidden, w_out):
    fetched, row_a, row_b = fetch(emb_table, requests, bag_rows, placement_slot)
    vectors = pool(row_a, row_b, fetched, w_hidden, w_out).reshape(N_DP, SHARD, VEC)
    vectors = lax.all_to_all(vectors, "dp", split_axis=0, concat_axis=0, tiled=True)
    return vectors.reshape(SLOTS, VEC)


def solution(mesh):
    placed = (
        P(("dp", "table"), None, None),
        P(("dp", "table"), None),
        P(("dp", "table")),
        P(("dp", "table")),
        P(),
        P(),
    )
    return jax.shard_map(
        local, mesh=mesh, in_specs=placed, out_specs=P(("dp", "table"), None), check_vma=False
    )
```

time: 590 us -> 295 us (0.50)
  Pallas kernels: 0 us -> 266 us
  local copies, waits for them, and re-layouts: 266 us -> 4.43 us
  waiting for transfers between devices: 168 us -> 0 us
  other arithmetic: 95.7 us -> 0 us
  starting transfers between devices: 20.5 us -> 0 us
  matrix products: 14.5 us -> 0 us
    pallas_call x0 -> x2, Pallas kernels: none -> 266 us  [the longest x1 156 us: fetch(): pl.pallas_call(fetch_kernel, in_specs=[hbm, vmem, vmem, vmem], out_specs=...]
    gather x5 -> x0, local copies, waits for them, and re-layouts: 248 us -> none  [the longest x1 224 us: local(): jnp.take(fetched_rows, slot_bags, axis=0)]
    all_to_all x2 -> x0, waiting for transfers between devices: 168 us -> none  [the longest x1 168 us: local(): lax.all_to_all(served, ('dp', 'table'), split_axis=0, concat_axis=0, tile...]
    reduce_sum x5 -> x0, other arithmetic: 72.1 us -> none  [the longest x1 64.3 us: local(): jnp.sum(picked, axis=2, dtype=jnp.float32).reshape(slot_count, width)]
    all_to_all x2 -> x0, starting transfers between devices: 20.5 us -> none  [the longest x1 10.3 us: local(): lax.all_to_all(requests, ('dp', 'table'), split_axis=0, concat_axis=0, ti...]
    dot_general x1 -> x0, matrix products: 14.5 us -> none  [item_tower(): raw = jnp.dot(hidden, w_out, preferred_element_type=jnp.float32)]
    select_n x4 -> x0, other arithmetic: 12.7 us -> none  [the longest x1 10.9 us: serve_local(): return jnp.where(live, served, jnp.zeros_like(served))]
    and x1 -> x0, local copies, waits for them, and re-layouts: 10.5 us -> none  [local(): jnp.take(fetched_rows, slot_bags, axis=0)]
  transfers between devices with their start and end apart: 2 -> 0, of which waited for: 1 -> 0; matrix products, arithmetic and copies ran while one was open for 8% -> 0% of each run, Pallas kernels for 0% -> 0%
where the time goes in v1:
time: 295 us; the launch traced here: 290 us
  Pallas kernels  266 us (90%)
  blocking collectives  19.6 us (7%)
  local copies, waits for them, and re-layouts  4.43 us (2%)
    pallas_call x1, Pallas kernels, fetch(): pl.pallas_call(fetch_kernel, in_specs=[hbm, vmem, vmem, vmem], out_specs=...  156 us
    pallas_call x1, Pallas kernels, pool(): pl.pallas_call(pool_kernel, grid=(N_DP,), in_specs=[smem, smem, pl.BlockS...  110 us
    all_to_all x1, blocking collectives, local(): lax.all_to_all(vectors, 'dp', split_axis=0, concat_axis=0, tiled=True)  19.6 us

profile of v1, /device:TPU:26, one launch (start us, length us, event | category | flops | bytes accessed | tf_op | source)
XLA Modules:
  0.0 290.3 jit_solution(4634103890571576924)
XLA Ops:
  0.0 0.8 copy.8
  0.8 2.0 reshape.17.placed
  2.8 0.6 pad.4
  3.5 156.4 %fetch_blocks.1 = (bf16[3,128,128,128]{3,2,1,0:T(8,128)(2,1)}, s32[256,128]{1,0:T(8,128)}, s32[256,128]{1,0:T(8,128)}) custom-call(bf16[256,128,128]{2,1,0:T(8,128)(2,1)} %emb.1, s32[128,1,128]{2,1,0:T(1,128)} %bitcast.7, s32[1024,128]{1,0:T(8,128)} %bitcast.6, s32[1024,4]{1,0:T(8,128)} %reshape.17.placed), custom_call_target="tpu_custom_call" | custom-call | tf_op jit(solution)/shard_map/fetch_blocks/pallas_call | solution.py:196
  159.9 109.8 %pool_and_tower.1 = bf16[2048,256]{1,0:T(8,128)(2,1)} custom-call(s32[256,128]{1,0:T(8,128)} %get-tuple-element.8.row_a, s32[256,128]{1,0:T(8,128)} %get-tuple-element.9.row_b, bf16[3,128,128,128]{3,2,1,0:T(8,128)(2,1)} %get-tuple-element.10.fetched, bf16[2048,1024]{1,0:T(8,128)(2,1)} %w_hidden.1, bf16[1024,256]{1,0:T(8,128)(2,1)} %w_out.1), custom_call_target="tpu_custom_call" | custom-call | tf_op jit(solution)/shard_map/pool_and_tower/pallas_call | solution.py:276
  269.7 19.6 %all_to_all.5 = bf16[8,256,256]{2,1,0:T(8,128)(2,1)S(1)} all-to-all(bf16[8,256,256]{2,1,0:T(8,128)(2,1)} %bitcast.4), channel_id=1, replica_groups=mesh['dp'=8,'table'=16] {'dp'}, dimensions={0} | all-to-all | bytes 2097152 | tf_op jit(solution)/shard_map/all_to_all | solution.py:303
  289.3 1.0 copy.10

commit v2 on v1

--- a/solution.py
+++ b/solution.py
@@ -25,6 +25,9 @@
 TABLE_ROWS = CAP * DEVICES * ROWS
 ZERO_ROW = TABLE_ROWS
 
+PHASES = 13
+SCHEDULE = (16, 32, 48, 80, 112, 112, 128, 144, 144, 160, 176, 192, GROUP)
+
 DISPLACEMENTS = [d for d in itertools.product(range(4), range(4), range(4), range(2)) if any(d)]
 
 
@@ -94,7 +97,8 @@
     part = ((dy - dx) & 3) * 2 + dcore
     place = part * 16 + dx * 4 + ((dz - dx) & 3)
     row = ((slot * DEVICES + place) << 7) | (idx & 127)
-    return jnp.where(present, row, ZERO_ROW), jnp.where(present, jnp.where(slot == 2, slot + part, slot), 0)
+    phase = jnp.where(slot == 2, 5 + part, jnp.where(slot == 1, 1 + (part >> 1), 0))
+    return jnp.where(present, row, ZERO_ROW), jnp.where(present, phase, 0)
 
 
 def pick_bags(bags_ref, placed_ref, bag_t, picked):
@@ -129,13 +133,33 @@
     return jnp.concatenate(rows), jnp.concatenate(live) > 0
 
 
-def fetch_kernel(
-    emb, req, bags, placed, fetched, row_a, row_b,
-    emb_v, staged, req_in, req_s, bag_t, picked,
-    emb_sem, req_send, req_recv, own_sem, send_sem, recv_sem,
+def sort_rows(key, load):
+    row = lax.broadcasted_iota(jnp.int32, (GROUP, GROUPS), 0)
+    size = 2
+    while size <= GROUP:
+        step = size // 2
+        while step:
+            lower = (row & step) == 0
+            other_key = jnp.where(lower, pltpu.roll(key, GROUP - step, 0), pltpu.roll(key, step, 0))
+            other_load = jnp.where(lower, pltpu.roll(load, GROUP - step, 0), pltpu.roll(load, step, 0))
+            keeps_least = lower == ((row & size) == 0)
+            swap = keeps_least == (other_key < key)
+            key = jnp.where(swap, other_key, key)
+            load = jnp.where(swap, other_load, load)
+            step //= 2
+        size *= 2
+    return key, load
+
+
+def fused_kernel(
+    emb, req, bags, placed, w_hidden, w_out,
+    out, fetched, row_a, row_b, late,
+    blocks, staged, table, req_in, req_s, bag_t, picked, sorted_a, sorted_b, order_t, rows_a, rows_b,
+    chunk, rows, x, vectors, flags,
+    emb_sem, req_send, req_recv, own_sem, send_sem, recv_sem, chunk_sem, flag_send, flag_recv, vec_send, vec_recv,
 ):
     me_dp, me_table = lax.axis_index("dp"), lax.axis_index("table")
-    load = pltpu.make_async_copy(emb, emb_v, emb_sem)
+    load = pltpu.make_async_copy(emb, blocks, emb_sem)
     load.start()
     barrier = pltpu.get_barrier_semaphore()
     for d in ORDER:
@@ -159,63 +183,249 @@
     load.wait()
     numbers.wait()
 
-    for slot in range(CAP):
+    def send(slot):
+        room = slot % 2
 
         def serve(n, _):
             number = req_s[n, 0, slot]
-            block = emb_v[jnp.maximum(number, 0)]
-            staged[slot, n] = jnp.where(number >= 0, block, jnp.zeros_like(block))
+            block = blocks[jnp.maximum(number, 0)]
+            staged[room, n] = jnp.where(number >= 0, block, jnp.zeros_like(block))
             return 0
 
         lax.fori_loop(0, DEVICES, serve, 0)
-        for d in ORDER if slot < 2 else ORDER_BY_PART:
+        for d in ORDER_BY_PART if slot else ORDER:
             n = place_of(d)
+            phase = (0, 1 + part_of(d) // 2, 5 + part_of(d))[slot]
             pltpu.make_async_remote_copy(
-                src_ref=staged.at[slot, n], dst_ref=fetched.at[slot, n],
-                send_sem=send_sem, recv_sem=recv_sem, device_id=moved(d, 1), device_id_type=MESH,
+                src_ref=staged.at[room, n], dst_ref=fetched.at[slot, n], send_sem=send_sem.at[slot],
+                recv_sem=recv_sem.at[phase], device_id=moved(d, 1), device_id_type=MESH,
             ).start()
-    mine = pltpu.make_async_copy(staged.at[:, 0], fetched.at[:, 0], own_sem)
-    mine.start()
-
+        mine = pltpu.make_async_copy(staged.at[room, 0], fetched.at[slot, 0], own_sem)
+        mine.start()
+        mine.wait()
+
+    def sent(slot):
+        room = staged.at[slot % 2, pl.ds(1, DEVICES - 1)]
+        pltpu.make_async_copy(room, room, send_sem.at[slot]).wait()
+
+    send(0)
+    send(1)
+
+    table[pl.ds(ZERO_ROW, 8), :] = jnp.zeros((8, EMB), jnp.float32)
     pick_bags(bags, placed, bag_t, picked)
-    for entry, out in ((0, row_a), (1, row_b)):
-        idx, present = bag_matrix(picked, entry)
-        out[...] = table_row(idx, present)[0]
-
-    mine.wait()
-    arrived = fetched.at[:, pl.ds(1, DEVICES - 1)]
-    pltpu.make_async_copy(arrived, arrived, recv_sem).wait()
-    sent = staged.at[:, pl.ds(1, DEVICES - 1)]
-    pltpu.make_async_copy(sent, sent, send_sem).wait()
-
-
-def fetch(emb_table, requests, bag_rows, placement_slot):
+    idx_a, present = bag_matrix(picked, 0)
+    idx_b, _ = bag_matrix(picked, 1)
+    idx_a, phase_a = table_row(idx_a, present)
+    idx_b, phase_b = table_row(idx_b, present)
+    row_a[...] = idx_a
+    row_b[...] = idx_b
+    row = lax.broadcasted_iota(jnp.int32, (GROUP, GROUPS), 0)
+    key = jnp.maximum(phase_a, phase_b) * GROUP + (row & 15) * 16 + (row >> 4)
+    key, pair = sort_rows(key, idx_a | (idx_b << 16))
+    sorted_a[...] = jnp.minimum(pair & 65535, ZERO_ROW)
+    sorted_b[...] = jnp.minimum((pair >> 16) & 65535, ZERO_ROW)
+    order_t[...] = jnp.transpose(key & (GROUP - 1))
+    to_a = pltpu.make_async_copy(sorted_a, rows_a, chunk_sem.at[0])
+    to_b = pltpu.make_async_copy(sorted_b, rows_b, chunk_sem.at[1])
+    to_a.start()
+    to_b.start()
+    limit = jnp.zeros_like(row)
+    for end in SCHEDULE[:-1]:
+        limit += jnp.where(row >= end, 1, 0)
+    missed = jnp.where((key >> 8) > limit, 1, 0)
+    flags[0] = jnp.broadcast_to(jnp.max(missed, axis=0, keepdims=True), (8, GROUPS))
+    to_a.wait()
+    to_b.wait()
+
+    def share(first, count, device):
+        copies = []
+        for s in range(1, count):
+            copies.append(
+                pltpu.make_async_remote_copy(
+                    src_ref=flags.at[first], dst_ref=flags.at[first + s], send_sem=flag_send.at[first + s],
+                    recv_sem=flag_recv.at[first + s], device_id=device(s), device_id_type=MESH,
+                )
+            )
+            copies[-1].start()
+        return copies
+
+    def gather_flags(copies, first, count):
+        for c in copies:
+            c.wait()
+        total = flags[first]
+        for s in range(1, count):
+            total = jnp.maximum(total, flags[first + s])
+        return total
+
+    def arrive(slot, first, count):
+        pieces = count // 16
+
+        def copy(n):
+            return pltpu.make_async_copy(
+                fetched.at[slot, pl.ds(first + n * 16, 16)], chunk.at[lax.rem(n, 2)], chunk_sem.at[lax.rem(n, 2)]
+            )
+
+        def convert(n):
+            copy(n).wait()
+            for k in range(16):
+                at = pl.multiple_of((slot * DEVICES + first + n * 16 + k) * ROWS, ROWS)
+                table[pl.ds(at, ROWS), :] = chunk[lax.rem(n, 2), k].astype(jnp.float32)
+
+        copy(0).start()
+
+        def piece(n, _):
+            copy(n + 1).start()
+            convert(n)
+            return 0
+
+        lax.fori_loop(0, pieces - 1, piece, 0)
+        convert(pieces - 1)
+
+    def add_rows(g, low, high, at):
+        for n in range(low, high):
+            a, b = rows_a[n, g], rows_b[n, g]
+            rows[at, n - low : n - low + 1, :] = table[pl.ds(a, 1), :] + table[pl.ds(b, 1), :]
+
+    def pool_some(low, high):
+        half, first = low // 128, low % 128
+        step = 2 if high - low < 32 else 1
+
+        def eight(n, _):
+            def one(m, _):
+                for k in range(step):
+                    add_rows(n * 8 + m * step + k, low, high, m * step + k)
+                return 0
+
+            lax.fori_loop(0, 8 // step, one, 0)
+            for m in range(8):
+                blocks[(n * 8 + m) * 2 + half, first : first + high - low, :] = rows[m, : high - low, :].astype(
+                    jnp.bfloat16
+                )
+            return 0
+
+        lax.fori_loop(0, GROUPS // 8, eight, 0)
+
+    def phase_done(phase):
+        if phase == 0:
+            slot, first, count = 0, 0, DEVICES
+        elif phase < 5:
+            slot, first, count = 1, (phase - 1) * 32, 32
+        else:
+            slot, first, count = 2, (phase - 5) * 16, 16
+        skip = 1 if first == 0 else 0
+        arrived = fetched.at[slot, pl.ds(first + skip, count - skip)]
+        pltpu.make_async_copy(arrived, arrived, recv_sem.at[phase]).wait()
+        arrive(slot, first, count)
+
+    flag_copies = share(0, N_DP, lambda s: (lax.rem(me_dp + s, N_DP), me_table))
+    done = 0
+    for phase in range(PHASES - 1):
+        phase_done(phase)
+        if phase == 0:
+            sent(0)
+            send(2)
+        if SCHEDULE[phase] > done:
+            pool_some(done, SCHEDULE[phase])
+            done = SCHEDULE[phase]
+    phase_done(PHASES - 1)
+    flags[8] = gather_flags(flag_copies, 0, N_DP)
+    flag_copies = share(8, N_TABLE, lambda s: (me_dp, lax.rem(me_table + s, N_TABLE)))
+
+    lane = lax.broadcasted_iota(jnp.int32, (GROUP, GROUP), 0)
+
+    def shard(s, _):
+        k = lax.rem(me_dp + 1 + s, N_DP)
+
+        def last_rows(n, _):
+            def one(m, _):
+                add_rows(k * 16 + n * 8 + m, done, GROUP, m)
+                return 0
+
+            lax.fori_loop(0, 8, one, 0)
+            for m in range(8):
+                blocks[(k * 16 + n * 8 + m) * 2 + 1, done - 128 :, :] = rows[m, : GROUP - done, :].astype(jnp.bfloat16)
+            return 0
+
+        lax.fori_loop(0, 2, last_rows, 0)
+
+        def in_place(n, _):
+            for m in range(4):
+                g = k * 16 + n * 4 + m
+                pick = jnp.where(order_t[pl.ds(g, 1), :] == lane, 1.0, 0.0).astype(jnp.bfloat16)
+                pooled = jnp.concatenate([blocks[2 * g], blocks[2 * g + 1]])
+                pooled = jnp.dot(pick, pooled, preferred_element_type=jnp.float32).astype(jnp.bfloat16)
+                at = pl.multiple_of((n * 4 + m) * 16, 16)
+                for f in range(FEATS):
+                    x[pl.ds(at, 16), f * EMB : (f + 1) * EMB] = pooled[f * 16 : (f + 1) * 16, :]
+            return 0
+
+        lax.fori_loop(0, 4, in_place, 0)
+        vectors[k] = tower(x[...], w_hidden[...], w_out[...])
+
+        @pl.when(s < N_DP - 1)
+        def _():
+            pltpu.make_async_remote_copy(
+                src_ref=vectors.at[k], dst_ref=out.at[me_dp], send_sem=vec_send.at[s],
+                recv_sem=vec_recv.at[me_dp], device_id=(k, me_table), device_id_type=MESH,
+            ).start()
+
+        return 0
+
+    lax.fori_loop(0, N_DP, shard, 0)
+    late[...] = gather_flags(flag_copies, 8, N_TABLE)
+    last = pltpu.make_async_copy(vectors.at[me_dp], out.at[me_dp], own_sem)
+    last.start()
+    sent(1)
+    sent(2)
+    for s in range(1, N_DP):
+        k = lax.rem(me_dp + s, N_DP)
+        pltpu.make_async_copy(vectors.at[k], vectors.at[k], vec_send.at[s - 1]).wait()
+        pltpu.make_async_copy(out.at[k], out.at[k], vec_recv.at[k]).wait()
+    last.wait()
+
+
+def fused(emb_table, requests, bag_rows, placement_slot, w_hidden, w_out):
     req = jnp.pad(requests, ((0, 0), (0, 125))).reshape(DEVICES, 1, 128)
     hbm = pl.BlockSpec(memory_space=pl.ANY)
     vmem = pl.BlockSpec(memory_space=pltpu.VMEM)
+    dma = pltpu.SemaphoreType.DMA
     return pl.pallas_call(
-        fetch_kernel,
-        in_specs=[hbm, vmem, vmem, vmem],
-        out_specs=(hbm, vmem, vmem),
+        fused_kernel,
+        in_specs=[hbm, vmem, vmem, vmem, vmem, vmem],
+        out_specs=(hbm, hbm, vmem, vmem, vmem),
         out_shape=(
+            jax.ShapeDtypeStruct((N_DP, SHARD, VEC), jnp.bfloat16),
             jax.ShapeDtypeStruct((CAP, DEVICES, ROWS, EMB), jnp.bfloat16),
             jax.ShapeDtypeStruct((GROUP, GROUPS), jnp.int32),
             jax.ShapeDtypeStruct((GROUP, GROUPS), jnp.int32),
+            jax.ShapeDtypeStruct((8, GROUPS), jnp.int32),
         ),
         scratch_shapes=[
             pltpu.VMEM((256, ROWS, EMB), jnp.bfloat16),
-            pltpu.VMEM((CAP, DEVICES, ROWS, EMB), jnp.bfloat16),
+            pltpu.VMEM((2, DEVICES, ROWS, EMB), jnp.bfloat16),
+            pltpu.VMEM((TABLE_ROWS + 8, EMB), jnp.float32),
             pltpu.VMEM((DEVICES, 1, 128), jnp.int32),
             pltpu.SMEM((DEVICES, 1, 128), jnp.int32),
             pltpu.VMEM((128, 1024), jnp.int32),
             pltpu.VMEM((16, 72, 128), jnp.float32),
-        ]
-        + [pltpu.SemaphoreType.DMA] * 6,
+            pltpu.VMEM((GROUP, GROUPS), jnp.int32),
+            pltpu.VMEM((GROUP, GROUPS), jnp.int32),
+            pltpu.VMEM((GROUPS, GROUP), jnp.int32),
+            pltpu.SMEM((GROUP, GROUPS), jnp.int32),
+            pltpu.SMEM((GROUP, GROUPS), jnp.int32),
+            pltpu.VMEM((2, 16, ROWS, EMB), jnp.bfloat16),
+            pltpu.VMEM((8, 96, EMB), jnp.float32),
+            pltpu.VMEM((SHARD, FEATS * EMB), jnp.bfloat16),
+            pltpu.VMEM((N_DP, SHARD, VEC), jnp.bfloat16),
+            pltpu.VMEM((24, 8, GROUPS), jnp.int32),
+            dma, dma, dma, dma, dma((CAP,)),
+            dma((PHASES,)), dma((2,)), dma((24,)), dma((24,)), dma((N_DP,)), dma((N_DP,)),
+        ],
         compiler_params=pltpu.CompilerParams(
-            collective_id=1, has_side_effects=True, vmem_limit_bytes=58 * 2**20
+            collective_id=1, has_side_effects=True, vmem_limit_bytes=59 * 2**20
         ),
-        name="fetch_blocks",
-    )(emb_table, req, bag_rows.reshape(1024, 128), placement_slot.reshape(1024, 4))
+        name="fetch_pool_and_tower",
+    )(emb_table, req, bag_rows.reshape(1024, 128), placement_slot.reshape(1024, 4), w_hidden, w_out)
 
 
 def tower(x, w_hidden, w_out):
@@ -298,9 +508,15 @@
 
 
 def local(emb_table, requests, bag_rows, placement_slot, w_hidden, w_out):
-    fetched, row_a, row_b = fetch(emb_table, requests, bag_rows, placement_slot)
-    vectors = pool(row_a, row_b, fetched, w_hidden, w_out).reshape(N_DP, SHARD, VEC)
-    vectors = lax.all_to_all(vectors, "dp", split_axis=0, concat_axis=0, tiled=True)
+    vectors, fetched, row_a, row_b, late = fused(
+        emb_table, requests, bag_rows, placement_slot, w_hidden, w_out
+    )
+
+    def general(vectors):
+        again = pool(row_a, row_b, fetched, w_hidden, w_out).reshape(N_DP, SHARD, VEC)
+        return lax.all_to_all(again, "dp", split_axis=0, concat_axis=0, tiled=True)
+
+    vectors = lax.cond(jnp.max(late) > 0, general, lambda vectors: vectors, vectors)
     return vectors.reshape(SLOTS, VEC)
 
 

time: 295 us -> 231 us (0.78); the launches traced: 290 us -> 230 us
  Pallas kernels: 266 us -> 224 us
  blocking collectives: 19.6 us -> 0 us
    pallas_call x2 -> x1, Pallas kernels: 266 us -> 224 us  [fused(): pl.pallas_call(fused_kernel, in_specs=[hbm, vmem, vmem, vmem, vmem, vmem]...]
    all_to_all x1 -> x0, blocking collectives: 19.6 us -> none  [local(): lax.all_to_all(vectors, 'dp', split_axis=0, concat_axis=0, tiled=True)]
where the time goes in v2:
time: 231 us; the launch traced here: 230 us
  Pallas kernels  224 us (97%)
  local copies, waits for them, and re-layouts  4.5 us (2%)
    pallas_call x1, Pallas kernels, fused(): pl.pallas_call(fused_kernel, in_specs=[hbm, vmem, vmem, vmem, vmem, vmem]...  224 us

profile of v2, /device:TPU:26, one launch (start us, length us, event | category | flops | bytes accessed | tf_op | source)
XLA Modules:
  0.0 230.4 jit_solution(7539221235985814824)
XLA Ops:
  0.0 0.0 copy-start
  0.0 0.8 copy.10
  0.8 0.6 pad.4
  1.5 2.0 reshape.21.placed
  3.5 223.9 %fetch_pool_and_tower.1 = (bf16[8,256,256]{2,1,0:T(8,128)(2,1)S(1)}, bf16[3,128,128,128]{3,2,1,0:T(8,128)(2,1)}, s32[256,128]{1,0:T(8,128)S(1)}, s32[256,128]{1,0:T(8,128)S(1)}, s32[8,128]{1,0:T(8,128)}) custom-call(bf16[256,128,128]{2,1,0:T(8,128)(2,1)} %emb.1, s32[128,1,128]{2,1,0:T(1,128)} %bitcast.9, s32[1024,128]{1,0:T(8,128)} %bitcast.8, ...), custom_call_target="tpu_custom_call" | custom-call | tf_op jit(solution)/shard_map/fetch_pool_and_tower/pallas_call | solution.py:392
  227.4 1.3 reduce_max.9
  229.4 0.0 copy-done
  229.4 1.0 copy.15
  (1 shorter events, 0.0 us)
Async XLA Ops:
  0.0 229.4 %copy-start = (bf16[1024,256]{1,0:T(8,128)(2,1)S(1)}, bf16[1024,256]{1,0:T(8,128)(2,1)}, u32[]{:S(2)}) copy-start(bf16[1024,256]{1,0:T(8,128)(2,1)} %w_out.1) | copy-start | bytes 1572868

commit v3 on v2

--- a/solution.py
+++ b/solution.py
@@ -209,7 +209,6 @@
         pltpu.make_async_copy(room, room, send_sem.at[slot]).wait()
 
     send(0)
-    send(1)
 
     table[pl.ds(ZERO_ROW, 8), :] = jnp.zeros((8, EMB), jnp.float32)
     pick_bags(bags, placed, bag_t, picked)
@@ -232,8 +231,9 @@
     limit = jnp.zeros_like(row)
     for end in SCHEDULE[:-1]:
         limit += jnp.where(row >= end, 1, 0)
-    missed = jnp.where((key >> 8) > limit, 1, 0)
-    flags[0] = jnp.broadcast_to(jnp.max(missed, axis=0, keepdims=True), (8, GROUPS))
+    missed = jnp.max(jnp.where((key >> 8) > limit, 1.0, 0.0), axis=0, keepdims=True)
+    missed = jnp.max(missed, axis=1, keepdims=True).astype(jnp.int32)
+    flags[0] = jnp.broadcast_to(missed, (8, GROUPS))
     to_a.wait()
     to_b.wait()
 
@@ -318,11 +318,12 @@
         arrive(slot, first, count)
 
     flag_copies = share(0, N_DP, lambda s: (lax.rem(me_dp + s, N_DP), me_table))
+    sent(0)
+    send(1)
     done = 0
     for phase in range(PHASES - 1):
         phase_done(phase)
         if phase == 0:
-            sent(0)
             send(2)
         if SCHEDULE[phase] > done:
             pool_some(done, SCHEDULE[phase])
@@ -349,17 +350,17 @@
         lax.fori_loop(0, 2, last_rows, 0)
 
         def in_place(n, _):
-            for m in range(4):
-                g = k * 16 + n * 4 + m
+            for m in range(8):
+                g = k * 16 + n * 8 + m
                 pick = jnp.where(order_t[pl.ds(g, 1), :] == lane, 1.0, 0.0).astype(jnp.bfloat16)
                 pooled = jnp.concatenate([blocks[2 * g], blocks[2 * g + 1]])
                 pooled = jnp.dot(pick, pooled, preferred_element_type=jnp.float32).astype(jnp.bfloat16)
-                at = pl.multiple_of((n * 4 + m) * 16, 16)
+                at = pl.multiple_of((n * 8 + m) * 16, 16)
                 for f in range(FEATS):
                     x[pl.ds(at, 16), f * EMB : (f + 1) * EMB] = pooled[f * 16 : (f + 1) * 16, :]
             return 0
 
-        lax.fori_loop(0, 4, in_place, 0)
+        lax.fori_loop(0, 2, in_place, 0)
         vectors[k] = tower(x[...], w_hidden[...], w_out[...])
 
         @pl.when(s < N_DP - 1)
@@ -516,7 +517,7 @@
         again = pool(row_a, row_b, fetched, w_hidden, w_out).reshape(N_DP, SHARD, VEC)
         return lax.all_to_all(again, "dp", split_axis=0, concat_axis=0, tiled=True)
 
-    vectors = lax.cond(jnp.max(late) > 0, general, lambda vectors: vectors, vectors)
+    vectors = lax.cond(late[0, 0] > 0, general, lambda vectors: vectors, vectors)
     return vectors.reshape(SLOTS, VEC)
 
 

time: 231 us -> 229 us (level)
  the two profiles are of different devices: /device:TPU:26 before, /device:TPU:125 now
where the time goes in v3:
time: 229 us; the launch traced here: 228 us
  Pallas kernels  221 us (97%)
  local copies, waits for them, and re-layouts  6.99 us (3%)
    pallas_call x1, Pallas kernels, fused(): pl.pallas_call(fused_kernel, in_specs=[hbm, vmem, vmem, vmem, vmem, vmem]...  221 us

profile of v3, /device:TPU:125, one launch (start us, length us, event | category | flops | bytes accessed | tf_op | source)
XLA Modules:
  0.0 228.4 jit_solution(4767314772816950577)
XLA Ops:
  0.0 0.0 copy-start.1
  0.0 0.8 copy.10
  0.8 0.6 pad.4
  1.5 2.0 reshape.25.placed
  3.5 0.0 copy-start
  3.5 220.7 %fetch_pool_and_tower.1 = (bf16[8,256,256]{2,1,0:T(8,128)(2,1)}, bf16[3,128,128,128]{3,2,1,0:T(8,128)(2,1)}, s32[256,128]{1,0:T(8,128)S(1)}, s32[256,128]{1,0:T(8,128)S(1)}, s32[8,128]{1,0:T(8,128)}) custom-call(bf16[256,128,128]{2,1,0:T(8,128)(2,1)} %emb.1, s32[128,1,128]{2,1,0:T(1,128)} %bitcast.10, s32[1024,128]{1,0:T(8,128)} %bitcast.9, ...), custom_call_target="tpu_custom_call" | custom-call | tf_op jit(solution)/shard_map/fetch_pool_and_tower/pallas_call | solution.py:393
  224.2 1.2 slice.3
  226.1 0.0 copy-done.1
  226.1 0.0 copy-done
  226.1 2.3 copy.15
  (1 shorter events, 0.0 us)
Async XLA Ops:
  0.0 226.1 %copy-start.1 = (bf16[1024,256]{1,0:T(8,128)(2,1)S(1)}, bf16[1024,256]{1,0:T(8,128)(2,1)}, u32[]{:S(2)}) copy-start(bf16[1024,256]{1,0:T(8,128)(2,1)} %w_out.1) | copy-start | bytes 1572868
  3.5 222.6 %copy-start = (bf16[2048,1024]{1,0:T(8,128)(2,1)S(1)}, bf16[2048,1024]{1,0:T(8,128)(2,1)}, u32[]{:S(2)}) copy-start(bf16[2048,1024]{1,0:T(8,128)(2,1)} %w_hidden.1) | copy-start | bytes 12582916
